TPU v7x, 32 devices: a whole 2x2x4 slice. The times are simulated.
32 devices in a mesh: parts: 2 (over x), space: 16 (over z, y, core).
Axes of the slice: x: 2, y: 2, z: 4, core: 2. Of those that a mesh axis runs over, the one named last changes fastest.
Arguments:
- vectors: bfloat16 [2, 12, 4, 3, 32, 8, 128], P(None, None, None, None, ('parts', 'space')), parts along dimension 4, may hold values from -6 to 6
- links: bfloat16 [2, 4, 3, 3, 32, 8, 128], P(None, None, None, None, ('parts', 'space')), parts along dimension 4, may hold values from -6 to 6
- clover: bfloat16 [2, 2, 6, 6, 32, 8, 128], P(None, None, None, None, ('parts', 'space')), parts along dimension 4, may hold values from -4 to 4
- block_owner: int32 [4096, 1], P(('parts', 'space')), parts along dimension 0, may hold values from 0 to 15; in each aligned block of 128 rows (0 to 127, 128 to 255, ...) at most 16 rows name the same one
- block_aggregate: int32 [4096], P(('parts', 'space')), parts along dimension 0, may hold values from 0 to 3
Outputs:
- applied: bfloat16 [2, 12, 4, 3, 32, 8, 128], P(None, None, None, None, ('parts', 'space')), parts along dimension 4
- coarse: float32 [128, 2, 12, 12], P(('parts', 'space')), parts along dimension 0
There are 2 independent parts, one for each index of `parts`. A program takes and returns all parts, laid end to end along the dimension named above; each array names one. Nothing has to cross between parts.
Inputs may be any that keep to these rules, and one draw needn't show every extreme that they name: `block_owner`: the 128 blocks of one device name one owner at most 16 times, and in every draw some device names some owner exactly 16 times.
All inputs are finite; a program needn't handle non-finite values.
Results may differ from a plain program's by a relative error of at most 0.003.
Values may be sent and summed in bfloat16 or wider, within the bound.
A program may use at most 192 MiB of HBM per device.

v0:
```python
import jax
import jax.numpy as jnp
import numpy as np
from jax import lax
from jax.sharding import PartitionSpec as P

VECTORS = 12
CZ = 8
CT = 16
AGG_DEV = 4
BLOCK_SITES = 8


def extended(x, sides, width):
    for axis, dim in sides:
        peers, length = (lax.axis_size(axis), x.shape[dim])
        up = [(i, (i + 1) % peers) for i in range(peers)]
        down = [(j, i) for i, j in up]
        last = lax.slice_in_dim(x, length - width, length, axis=dim)
        leading = lax.slice_in_dim(x, 0, width, axis=dim)
        before = lax.ppermute(last, axis, up)
        after = lax.ppermute(leading, axis, down)
        x = jnp.concatenate([before, x, after], axis=dim)
    return x


def passed_along(block, axis, distance):
    devices = range(lax.axis_size(axis))
    route = [((i - distance) % len(devices), i) for i in devices]
    return lax.ppermute(block, axis, route)


def block_four(upper_left, upper_right, lower_left, lower_right):
    rows = [list(upper_left[i]) + list(upper_right[i]) for i in range(2)]
    rows = rows + [list(lower_left[i]) + list(lower_right[i]) for i in range(2)]
    return np.array(rows, dtype=complex)


def two_on_two(upper, lower):
    rows = [list(upper[i]) for i in range(2)] + [list(lower[i]) for i in range(2)]
    return np.array(rows, dtype=complex)


def spin_tables():
    pauli_list = [
        np.array([[0, 1], [1, 0]], dtype=complex),
        np.array([[0, -1j], [1j, 0]], dtype=complex),
        np.array([[1, 0], [0, -1]], dtype=complex),
    ]
    zeros_two = np.zeros((2, 2), dtype=complex)
    ident_two = np.eye(2, dtype=complex)
    gammas = [block_four(zeros_two, -1j * pauli, 1j * pauli, zeros_two) for pauli in pauli_list]
    gammas.append(block_four(zeros_two, ident_two, ident_two, zeros_two))
    minus_proj = np.stack([(np.eye(4) - gamma)[:2, :] for gamma in gammas])
    plus_proj = np.stack([(np.eye(4) + gamma)[:2, :] for gamma in gammas])
    minus_back = np.stack([two_on_two(ident_two, -gamma[2:, :2]) for gamma in gammas])
    plus_back = np.stack([two_on_two(ident_two, gamma[2:, :2]) for gamma in gammas])
    tables = []
    for table in (minus_proj, plus_proj, minus_back, plus_back):
        tables.append((table.real.astype(np.float32), table.imag.astype(np.float32)))
    return tables


def contract(form, left, right):
    return jnp.einsum(form, left, right, precision=lax.Precision.HIGHEST)


def color_apply(link_real, link_imag, field_real, field_imag, dagger):
    if dagger:
        form = "baxyz,...sbxyz->...saxyz"
        twisted_imag = -link_imag
    else:
        form = "abxyz,...sbxyz->...saxyz"
        twisted_imag = link_imag
    out_real = contract(form, link_real, field_real) - contract(form, twisted_imag, field_imag)
    out_imag = contract(form, link_real, field_imag) + contract(form, twisted_imag, field_real)
    return (out_real, out_imag)


def spin_apply(table_real, table_imag, field_real, field_imag):
    form = "st,...taxyz->...saxyz"
    table_real = jnp.asarray(table_real)
    table_imag = jnp.asarray(table_imag)
    out_real = contract(form, table_real, field_real) - contract(form, table_imag, field_imag)
    out_imag = contract(form, table_real, field_imag) + contract(form, table_imag, field_real)
    return (out_real, out_imag)


def to_half(real_part, imag_part):
    stacked = jnp.stack([real_part, imag_part]).astype(jnp.bfloat16)
    stacked = lax.optimization_barrier(stacked)
    wide = stacked.astype(jnp.float32)
    return (wide[0], wide[1])


def lower_half(direction, field_real, field_imag):
    tables = spin_tables()
    proj_real, proj_imag = tables[0]
    out_real, out_imag = spin_apply(
        proj_real[direction], proj_imag[direction], field_real, field_imag
    )
    return to_half(out_real, out_imag)


def upper_half(direction, link_real, link_imag, field_real, field_imag):
    tables = spin_tables()
    proj_real, proj_imag = tables[1]
    out_real, out_imag = spin_apply(
        proj_real[direction], proj_imag[direction], field_real, field_imag
    )
    out_real, out_imag = color_apply(link_real, link_imag, out_real, out_imag, True)
    return to_half(out_real, out_imag)


def move(field, direction, step):
    if direction == 1:
        return jnp.roll(field, -step, axis=-2)
    shape = field.shape
    split = field.reshape(shape[:-1] + (CZ, CT))
    if direction == 2:
        rolled = jnp.roll(split, -step, axis=-2)
    else:
        rolled = jnp.roll(split, -step, axis=-1)
        times = jnp.arange(CT)
        edge = CT - 1 if step > 0 else 0
        rolled = jnp.where(times == edge, -rolled, rolled)
    return rolled.reshape(shape)


def clover_apply(clover_real, clover_imag, field_real, field_imag):
    shape = field_real.shape
    paired = shape[:-5] + (2, 6) + shape[-3:]
    form = "hijxyz,...hjxyz->...hixyz"
    left_real = field_real.reshape(paired)
    left_imag = field_imag.reshape(paired)
    out_real = contract(form, clover_real, left_real) - contract(form, clover_imag, left_imag)
    out_imag = contract(form, clover_real, left_imag) + contract(form, clover_imag, left_real)
    return (out_real.reshape(shape), out_imag.reshape(shape))


def operator(
    field_real, field_imag, links_real, links_imag, clover_real, clover_imag, ahead_x, behind_x
):
    tables = spin_tables()
    minus_real, minus_imag = tables[2]
    plus_real, plus_imag = tables[3]
    local_real, local_imag = clover_apply(clover_real, clover_imag, field_real, field_imag)
    total_real = 4.0 * field_real + local_real
    total_imag = 4.0 * field_imag + local_imag
    for direction in range(4):
        if direction == 0:
            ahead = ahead_x
            behind = behind_x
        else:
            lowered = lower_half(direction, field_real, field_imag)
            raised = upper_half(
                direction, links_real[direction], links_imag[direction], field_real, field_imag
            )
            ahead = (move(lowered[0], direction, 1), move(lowered[1], direction, 1))
            behind = (move(raised[0], direction, -1), move(raised[1], direction, -1))
        forward = color_apply(
            links_real[direction], links_imag[direction], ahead[0], ahead[1], False
        )
        forward = spin_apply(minus_real[direction], minus_imag[direction], forward[0], forward[1])
        backward = spin_apply(plus_real[direction], plus_imag[direction], behind[0], behind[1])
        total_real = total_real - 0.5 * (forward[0] + backward[0])
        total_imag = total_imag - 0.5 * (forward[1] + backward[1])
    return (total_real, total_imag)


def body(vectors, links, clover, block_owner, block_aggregate):
    links_wide = links.astype(jnp.float32)
    clover_wide = clover.astype(jnp.float32)
    center = vectors.astype(jnp.float32)
    padded = extended(vectors, (("space", 4),), 1)
    link_top = links[:, 0, :, :, -1:, :, :]
    link_below = passed_along(link_top, "space", 1)
    link_column = jnp.concatenate([link_below, links[:, 0, :, :, :-1, :, :]], axis=3).astype(
        jnp.float32
    )
    ahead_wide = padded[:, :, :, :, 2:, :, :].astype(jnp.float32)
    behind_wide = padded[:, :, :, :, :-2, :, :].astype(jnp.float32)
    ahead_x = lower_half(0, ahead_wide[0], ahead_wide[1])
    behind_x = upper_half(0, link_column[0], link_column[1], behind_wide[0], behind_wide[1])
    out_real, out_imag = operator(
        center[0],
        center[1],
        links_wide[0],
        links_wide[1],
        clover_wide[0],
        clover_wide[1],
        ahead_x,
        behind_x,
    )
    applied = jnp.stack([out_real, out_imag]).astype(jnp.bfloat16)
    form = "ksaxyn,jsaxyn->kjn"
    sum_real = jnp.einsum(
        form, vectors[0], applied[0], preferred_element_type=jnp.float32
    ) + jnp.einsum(form, vectors[1], applied[1], preferred_element_type=jnp.float32)
    sum_imag = jnp.einsum(
        form, vectors[0], applied[1], preferred_element_type=jnp.float32
    ) - jnp.einsum(form, vectors[1], applied[0], preferred_element_type=jnp.float32)
    block_count = sum_real.shape[-1]
    block_terms = jnp.transpose(jnp.stack([sum_real, sum_imag]), (3, 0, 1, 2)).reshape(
        block_count, -1
    )
    owners = block_owner[:, 0]
    targets = owners * AGG_DEV + block_aggregate
    wanted = jnp.arange(AGG_DEV * lax.axis_size("space"), dtype=jnp.int32)
    select = (targets[None, :] == wanted[:, None]).astype(jnp.float32)
    summed = lax.psum_scatter(
        jnp.dot(select, block_terms, precision=lax.Precision.HIGHEST),
        "space",
        scatter_dimension=0,
        tiled=True,
    )
    coarse = summed / (12.0 * BLOCK_SITES)
    return (applied, coarse.reshape(AGG_DEV, 2, VECTORS, VECTORS))


def solution(mesh):
    return jax.shard_map(
        body,
        mesh=mesh,
        in_specs=(
            P(None, None, None, None, ("parts", "space"), None, None),
            P(None, None, None, None, ("parts", "space"), None, None),
            P(None, None, None, None, ("parts", "space"), None, None),
            P(("parts", "space"), None),
            P(("parts", "space")),
        ),
        out_specs=(
            P(None, None, None, None, ("parts", "space"), None, None),
            P(("parts", "space"), None, None, None),
        ),
        check_vma=False,
    )
```

profile of v0, /device:TPU:0, one launch (start us, length us, event | category | flops | bytes accessed | tf_op | source)
XLA Modules:
  0.0 777.3 jit_solution(1158870131117473268)
XLA Ops:
  51.9 10.2 %fusion.32 = bf16[1,12,2,3,1,8,128]{1,3,2,6,5,4,0:T(4,128)(2,1)} fusion(f32[8,128,12,2,3]{2,4,3,1,0:T(4,128)S(1)} %fusion.134, f32[12,2,3,8,128]{0,2,1,4,3:T(4,128)S(1)} %copy-done, f32[1,1,3,3,1,8,128]{2,3,6,5,4,1,0:T(4,128)S(1)} %copy.545), kind=kOutput, calls=%fused_computation.56 | convolution fusion | flops 2801664 | bytes 774144 | tf_op jit(solution)/shard_map/baxyz,...sbxyz->...saxyz/dot_general | solution.py:65
  64.5 12.1 %fusion.35 = bf16[1,12,2,3,1,8,128]{1,3,2,6,5,4,0:T(4,128)(2,1)} fusion(f32[8,128,12,2,3]{2,4,3,1,0:T(4,128)} %fusion.132, f32[12,2,3,8,128]{0,2,1,4,3:T(4,128)} %copy.388, f32[1,1,3,3,1,8,128]{2,3,6,5,4,1,0:T(4,128)S(1)} %copy.545), kind=kOutput, calls=%fused_computation.57 | convolution fusion | flops 2801664 | bytes 774144 | tf_op jit(solution)/shard_map/baxyz,...sbxyz->...saxyz/dot_general | solution.py:65
  120.0 9.0 %fusion.138 = f32[8,128,12,2,3]{2,4,3,1,0:T(4,128)} fusion(f32[12,2,3,8,128]{0,2,1,4,3:T(4,128)} %copy.381, bf16[1,1,3,3,1,8,128]{3,2,6,5,4,1,0:T(4,128)(2,1)S(1)} %copy.530), kind=kOutput, calls=%fused_computation.186 | convolution fusion | flops 2654208 | bytes 608256 | tf_op jit(solution)/shard_map/abxyz,...sbxyz->...saxyz/dot_general | solution.py:65
  133.3 9.1 %fusion.136 = f32[8,128,12,2,3]{2,4,3,1,0:T(4,128)} fusion(f32[12,2,3,8,128]{0,2,1,4,3:T(4,128)} %copy.383, bf16[1,1,3,3,1,8,128]{3,2,6,5,4,1,0:T(4,128)(2,1)S(1)} %copy.530), kind=kOutput, calls=%fused_computation.184 | convolution fusion | flops 2654208 | bytes 608256 | tf_op jit(solution)/shard_map/abxyz,...sbxyz->...saxyz/dot_general | solution.py:65
  153.7 10.5 %add_bitcast_fusion.3 = f32[12,2,3,8,128]{0,2,1,4,3:T(4,128)} fusion(f32[8,128,12,2,3]{2,4,3,1,0:T(4,128)} %fusion.136, f32[12,2,3,8,128]{0,2,1,4,3:T(4,128)} %copy.381, bf16[1,1,3,3,1,8,128]{3,2,6,5,4,1,0:T(4,128)(2,1)S(1)} %copy.531), kind=kOutput, calls=%fused_computation.22 | convolution fusion | flops 2727936 | bytes 903168 | tf_op jit(solution)/shard_map/abxyz,...sbxyz->...saxyz/dot_general | solution.py:65
  186.7 7.1 fusion.128
  211.5 10.5 %add_bitcast_fusion.2 = f32[12,2,3,8,128]{0,2,1,4,3:T(4,128)} fusion(f32[8,128,12,2,3]{2,4,3,1,0:T(4,128)} %fusion.126, f32[12,2,3,8,128]{0,2,1,4,3:T(4,128)} %bitcast.829, bf16[1,1,3,3,1,8,128]{3,2,6,5,4,1,0:T(4,128)(2,1)S(1)} %copy.533), kind=kOutput, calls=%fused_computation.18 | convolution fusion | flops 2727936 | bytes 903168 | tf_op jit(solution)/shard_map/abxyz,...sbxyz->...saxyz/dot_general | solution.py:65
  229.6 7.9 %fusion.124 = f32[8,128,12,2,3]{2,4,3,1,0:T(4,128)} fusion(f32[12,2,3,8,128]{0,2,1,4,3:T(4,128)} %copy.404, bf16[1,1,3,3,1,8,128]{3,2,6,5,4,1,0:T(4,128)(2,1)S(1)} %copy.532), kind=kOutput, calls=%fused_computation.172 | convolution fusion | flops 2654208 | bytes 608256 | tf_op jit(solution)/shard_map/baxyz,...sbxyz->...saxyz/dot_general | solution.py:65
  241.4 8.1 %fusion.122 = f32[8,128,12,2,3]{2,4,3,1,0:T(4,128)} fusion(f32[12,2,3,8,128]{0,2,1,4,3:T(4,128)} %copy.407, bf16[1,1,3,3,1,8,128]{3,2,6,5,4,1,0:T(4,128)(2,1)S(1)} %copy.532), kind=kOutput, calls=%fused_computation.170 | convolution fusion | flops 2654208 | bytes 608256 | tf_op jit(solution)/shard_map/baxyz,...sbxyz->...saxyz/dot_general | solution.py:65
  249.5 10.4 %fusion.38 = bf16[1,12,2,3,1,8,128]{1,3,2,6,5,4,0:T(4,128)(2,1)} fusion(f32[8,128,12,2,3]{2,4,3,1,0:T(4,128)S(1)} %copy-done.12, f32[12,2,3,8,128]{0,2,1,4,3:T(4,128)S(1)} %copy-done.1, f32[1,1,3,3,1,8,128]{2,3,6,5,4,1,0:T(4,128)S(1)} %copy.546), kind=kOutput, calls=%fused_computation.58 | convolution fusion | flops 2801664 | bytes 774144 | tf_op jit(solution)/shard_map/baxyz,...sbxyz->...saxyz/dot_general | solution.py:65
  262.2 11.9 %fusion.41 = bf16[1,12,2,3,1,8,128]{1,3,2,6,5,4,0:T(4,128)(2,1)} fusion(f32[8,128,12,2,3]{2,4,3,1,0:T(4,128)} %fusion.122, f32[12,2,3,8,128]{0,2,1,4,3:T(4,128)} %copy.404, f32[1,1,3,3,1,8,128]{2,3,6,5,4,1,0:T(4,128)S(1)} %copy.546), kind=kOutput, calls=%fused_computation.59 | convolution fusion | flops 2801664 | bytes 774144 | tf_op jit(solution)/shard_map/baxyz,...sbxyz->...saxyz/dot_general | solution.py:65
  296.0 7.0 fusion.116
  309.6 10.6 %fusion.44 = bf16[1,12,2,3,1,8,128]{1,3,2,6,5,4,0:T(4,128)(2,1)} fusion(f32[8,128,12,2,3]{2,4,3,1,0:T(4,128)S(1)} %fusion.116, f32[12,2,3,8,128]{0,2,1,4,3:T(4,128)S(1)} %copy-done.2, f32[1,1,3,3,1,8,128]{2,3,6,5,4,1,0:T(4,128)S(1)} %copy.547), kind=kOutput, calls=%fused_computation.60 | convolution fusion | flops 2801664 | bytes 774144 | tf_op jit(solution)/shard_map/baxyz,...sbxyz->...saxyz/dot_general | solution.py:65
  322.5 11.9 %fusion.47 = bf16[1,12,2,3,1,8,128]{1,3,2,6,5,4,0:T(4,128)(2,1)} fusion(f32[8,128,12,2,3]{2,4,3,1,0:T(4,128)} %fusion.114, f32[12,2,3,8,128]{0,2,1,4,3:T(4,128)} %copy.423, f32[1,1,3,3,1,8,128]{2,3,6,5,4,1,0:T(4,128)S(1)} %copy.547), kind=kOutput, calls=%fused_computation.61 | convolution fusion | flops 2801664 | bytes 774144 | tf_op jit(solution)/shard_map/baxyz,...sbxyz->...saxyz/dot_general | solution.py:65
  370.2 7.8 %fusion.13 = f32[8,128,12,2,3]{2,4,3,1,0:T(4,128)S(1)} fusion(f32[12,2,3,8,128]{0,2,1,4,3:T(4,128)} %bitcast.826, pred[128]{0:T(512)(128)(4,1)S(1)} %broadcast_in_dim.32, bf16[1,1,3,3,1,8,128]{3,2,6,5,4,1,0:T(4,128)(2,1)S(1)} %copy.538), kind=kOutput, calls=%fused_computation.29 | convolution fusion | flops 2801664 | bytes 608384 | tf_op jit(solution)/shard_map/abxyz,...sbxyz->...saxyz/dot_general | solution.py:65
  378.0 7.0 fusion.12
  385.0 8.3 %subtract_bitcast_fusion.1 = f32[12,2,3,8,128]{0,2,1,4,3:T(4,128)} fusion(f32[8,128,12,2,3]{2,4,3,1,0:T(4,128)S(1)} %fusion.13, f32[12,2,3,8,128]{0,2,1,4,3:T(4,128)S(1)} %bitcast.833, pred[128]{0:T(512)(128)(4,1)S(1)} %broadcast_in_dim.32, bf16[1,1,3,3,1,8,128]{3,2,6,5,4,1,0:T(4,128)(2,1)S(1)} %copy.539), kind=kOutput, calls=%fused_computation.15 | convolution fusion | flops 2875392 | bytes 903296 | tf_op jit(solution)/shard_map/abxyz,...sbxyz->...saxyz/dot_general | solution.py:65
  396.7 11.5 %add_bitcast_fusion.1 = f32[12,2,3,8,128]{0,2,1,4,3:T(4,128)} fusion(f32[8,128,12,2,3]{2,4,3,1,0:T(4,128)} %fusion.12, f32[12,2,3,8,128]{0,2,1,4,3:T(4,128)} %bitcast.832, pred[128]{0:T(512)(128)(4,1)S(1)} %broadcast_in_dim.32, bf16[1,1,3,3,1,8,128]{3,2,6,5,4,1,0:T(4,128)(2,1)S(1)} %copy.538), kind=kOutput, calls=%fused_computation.14 | convolution fusion | flops 2875392 | bytes 903296 | tf_op jit(solution)/shard_map/abxyz,...sbxyz->...saxyz/dot_general | solution.py:65
  469.8 10.4 %subtract_bitcast_fusion = f32[12,2,6,1,8,128]{0,2,5,4,1,3:T(8,128)} fusion(f32[2,8,128,12,6]{3,4,2,1,0:T(8,128)} %fusion.2, bf16[12,2,6,8,128]{0,2,4,3,1:T(8,128)(2,1)} %copy.352, bf16[1,2,6,6,1,8,128]{3,2,6,5,1,4,0:T(8,128)(2,1)S(1)} %copy-done.9), kind=kOutput, calls=%fused_computation.1 | convolution fusion | flops 1916928 | bytes 1622016 | tf_op jit(solution)/shard_map/hijxyz,...hjxyz->...hixyz/dot_general | solution.py:65
  480.2 9.2 %add_bitcast_fusion = f32[12,2,6,1,8,128]{0,2,5,4,1,3:T(8,128)} fusion(f32[2,8,128,12,6]{3,4,2,1,0:T(8,128)} %fusion, bf16[12,2,6,8,128]{0,2,4,3,1:T(8,128)(2,1)S(1)} %copy-done.7, bf16[1,2,6,6,1,8,128]{3,2,6,5,1,4,0:T(8,128)(2,1)S(1)} %copy-done.9), kind=kOutput, calls=%fused_computation | convolution fusion | flops 1916928 | bytes 1622016 | tf_op jit(solution)/shard_map/hijxyz,...hjxyz->...hixyz/dot_general | solution.py:65
  592.0 11.2 %fusion.24 = f32[8,128,12,2,3]{2,4,3,1,0:T(4,128)S(1)} fusion(f32[12,2,3,8,128]{0,2,1,4,3:T(4,128)} %copy.373, f32[1,3,3,1,8,128]{1,2,5,4,3,0:T(4,128)} %copy.544), kind=kOutput, calls=%fused_computation.48 | convolution fusion | flops 2654208 | bytes 626688 | tf_op jit(solution)/shard_map/baxyz,...sbxyz->...saxyz/dot_general | solution.py:65
  603.2 9.7 %fusion.22 = f32[8,128,12,2,3]{2,4,3,1,0:T(4,128)} fusion(f32[12,2,3,8,128]{0,2,1,4,3:T(4,128)S(1)} %copy-done.6, f32[1,3,3,1,8,128]{1,2,5,4,3,0:T(4,128)S(1)} %copy-done.16), kind=kOutput, calls=%fused_computation.46 | convolution fusion | flops 2654208 | bytes 626688 | tf_op jit(solution)/shard_map/baxyz,...sbxyz->...saxyz/dot_general | solution.py:65
  622.6 10.4 %fusion.31 = bf16[1,12,2,3,1,8,128]{1,3,2,6,5,4,0:T(4,128)(2,1)} fusion(f32[8,128,12,2,3]{2,4,3,1,0:T(4,128)} %fusion.22, f32[12,2,3,8,128]{0,2,1,4,3:T(4,128)} %copy.373, bf16[1,3,3,1,8,128]{1,2,5,4,3,0:T(4,128)(2,1)} %copy.527), kind=kOutput, calls=%fused_computation.55 | convolution fusion | flops 2801664 | bytes 755712 | tf_op jit(solution)/shard_map/baxyz,...sbxyz->...saxyz/dot_general | solution.py:65
  682.3 86.5 %all-reduce.3.cloned.1.call-done = f32[64,288]{1,0:T(8,128)} async-done(((f32[64,288]{1,0:T(8,128)}), f32[64,288]{1,0:T(8,128)}) %all-reduce.3.cloned.1.call-update) | async-done | bytes 73744
  (450 shorter events, 452.4 us)
Async XLA Ops:
  7.2 14.7 %copy-start.111 = (f32[2,4,1,1,1]{1,0,4,3,2:T(2,128)S(1)}, f32[2,4,1,1,1]{1,0,4,3,2:T(2,128)}, u32[]{:S(2)}) copy-start(f32[2,4,1,1,1]{1,0,4,3,2:T(2,128)} %constant.104) | copy-start | bytes 100
  7.2 17.7 %copy-start.58 = (bf16[2,4,3,3,1,8,128]{6,5,4,3,2,1,0:T(8,128)(2,1)S(1)}, bf16[2,4,3,3,1,8,128]{6,5,4,3,2,1,0:T(8,128)(2,1)}, u32[]{:S(2)}) copy-start(bf16[2,4,3,3,1,8,128]{6,5,4,3,2,1,0:T(8,128)(2,1)} %param.38) | copy-start | bytes 442372
  7.2 761.6 %all-reduce.3.cloned.1.call-start = ((), (), s32[]{:S(2)}) async-start(), calls=%async_computation | async-start | bytes 196608
  10.0 16.4 %copy-start.110 = (f32[2,4,1,1,1]{1,0,4,3,2:T(2,128)S(1)}, f32[2,4,1,1,1]{1,0,4,3,2:T(2,128)}, u32[]{:S(2)}) copy-start(f32[2,4,1,1,1]{1,0,4,3,2:T(2,128)} %constant.107) | copy-start | bytes 100
  10.0 528.1 %collective-permute-start = (bf16[2,12,4,3,1,8,128]{6,2,5,3,1,4,0:T(4,128)(2,1)}, bf16[2,12,4,3,1,8,128]{6,2,5,3,1,4,0:T(4,128)(2,1)}, u32[]{:S(2)}, u32[]{:S(2)}) collective-permute-start(bf16[2,12,4,3,1,8,128]{6,2,5,3,1,4,0:T(4,128)(2,1)} %get-tuple-element.15), channel_id=1, source_target_pairs={{1,0},{2,1},{3,2},{4,3},{5,4},{6,5},{7,6},{8,7},{9,8},{10,9},{11,1... | collective-permute-start | bytes 1769480 | tf_op jit(solution)/shard_map/ppermute | solution.py:22
  15.4 559.5 %collective-permute-start.1 = (bf16[2,12,4,3,1,8,128]{6,2,5,3,1,4,0:T(4,128)(2,1)}, bf16[2,12,4,3,1,8,128]{6,2,5,3,1,4,0:T(4,128)(2,1)}, u32[]{:S(2)}, u32[]{:S(2)}) collective-permute-start(bf16[2,12,4,3,1,8,128]{6,2,5,3,1,4,0:T(4,128)(2,1)} %get-tuple-element.15), channel_id=1, source_target_pairs={{0,1},{1,2},{2,3},{3,4},{4,5},{5,6},{6,7},{7,8},{8,9},{9,10},{10,1... | collective-permute-start | bytes 1769480 | tf_op jit(solution)/shard_map/ppermute | solution.py:21
  16.8 516.3 %collective-permute-start.2 = (bf16[2,3,3,1,8,128]{5,4,3,2,1,0:T(8,128)(2,1)}, bf16[2,3,3,1,8,128]{5,4,3,2,1,0:T(8,128)(2,1)}, u32[]{:S(2)}, u32[]{:S(2)}) collective-permute-start(bf16[2,3,3,1,8,128]{5,4,3,2,1,0:T(8,128)(2,1)} %slice_bitcast_fusion.18), channel_id=1, source_target_pairs={{15,0},{0,1},{1,2},{2,3},{3,4},{4,5},{5,6},{6,7},{7,8},{8,9},{9,10... | collective-permute-start | bytes 110600 | tf_op jit(solution)/shard_map/ppermute | solution.py:30
  97.2 12.1 %copy-start.106 = (f32[2,4,1,1,1]{1,0,4,3,2:T(2,128)S(1)}, f32[2,4,1,1,1]{1,0,4,3,2:T(2,128)}, u32[]{:S(2)}) copy-start(f32[2,4,1,1,1]{1,0,4,3,2:T(2,128)} %constant.116) | copy-start | bytes 100
  100.8 16.0 %copy-start.56 = (f32[12,2,3,1,7,128]{5,1,4,2,0,3:T(2,128)S(1)}, f32[12,2,3,1,7,128]{5,1,4,2,0,3:T(2,128)}, u32[]{:S(2)}) copy-start(f32[12,2,3,1,7,128]{5,1,4,2,0,3:T(2,128)} %slice.319) | copy-start | bytes 774148
  417.4 32.2 %copy-start.51 = (f32[12,2,3,8,128]{4,3,2,1,0:T(8,128)}, f32[12,2,3,8,128]{4,3,2,1,0:T(8,128)S(1)}, u32[]{:S(2)}) copy-start(f32[12,2,3,8,128]{4,3,2,1,0:T(8,128)S(1)} %reshape.1176) | copy-start | bytes 884740
  433.0 12.3 %copy-start.31 = (f32[12,2,3,8,128]{4,3,2,1,0:T(8,128)S(1)}, f32[12,2,3,8,128]{4,3,2,1,0:T(8,128)}, u32[]{:S(2)}) copy-start(f32[12,2,3,8,128]{4,3,2,1,0:T(8,128)} %reshape.1179) | copy-start | bytes 884740
  435.0 12.5 %copy-start.49 = (f32[12,2,3,8,128]{4,3,2,1,0:T(8,128)S(1)}, f32[12,2,3,8,128]{4,3,2,1,0:T(8,128)}, u32[]{:S(2)}) copy-start(f32[12,2,3,8,128]{4,3,2,1,0:T(8,128)} %reshape.1175) | copy-start | bytes 884740
  435.0 12.5 %copy-start.100 = (pred[128]{0:T(512)(128)(4,1)S(1)}, pred[128]{0:T(512)(128)(4,1)}, u32[]{:S(2)}) copy-start(pred[128]{0:T(512)(128)(4,1)} %broadcast_in_dim.35) | copy-start | bytes 388
  435.0 12.5 %copy-start.105 = (f32[4,2,1,1,1]{0,1,4,3,2:T(2,128)S(1)}, f32[4,2,1,1,1]{0,1,4,3,2:T(2,128)}, u32[]{:S(2)}) copy-start(f32[4,2,1,1,1]{0,1,4,3,2:T(2,128)} %constant.120) | copy-start | bytes 100
  437.1 14.6 %copy-start.96 = (f32[4,2,1,1,1]{0,1,4,3,2:T(2,128)S(1)}, f32[4,2,1,1,1]{0,1,4,3,2:T(2,128)}, u32[]{:S(2)}) copy-start(f32[4,2,1,1,1]{0,1,4,3,2:T(2,128)} %constant.117) | copy-start | bytes 100
  439.4 14.6 %copy-start.91 = (f32[4,2,1,1,1]{0,1,4,3,2:T(2,128)S(1)}, f32[4,2,1,1,1]{0,1,4,3,2:T(2,128)}, u32[]{:S(2)}) copy-start(f32[4,2,1,1,1]{0,1,4,3,2:T(2,128)} %constant.118) | copy-start | bytes 100
  443.4 14.7 %copy-start.7 = (bf16[12,2,6,8,128]{0,2,4,3,1:T(8,128)(2,1)S(1)}, bf16[12,2,6,8,128]{0,2,4,3,1:T(8,128)(2,1)}, u32[]{:S(2)}) copy-start(bf16[12,2,6,8,128]{0,2,4,3,1:T(8,128)(2,1)} %copy.356) | copy-start | bytes 884740
  443.4 14.7 %copy-start.8 = (bf16[1,2,6,6,1,8,128]{3,2,6,5,1,4,0:T(8,128)(2,1)S(1)}, bf16[1,2,6,6,1,8,128]{3,2,6,5,1,4,0:T(8,128)(2,1)}, u32[]{:S(2)}) copy-start(bf16[1,2,6,6,1,8,128]{3,2,6,5,1,4,0:T(8,128)(2,1)} %copy.523) | copy-start | bytes 442372
  480.2 12.7 %copy-start.46 = (f32[12,2,3,1,7,128]{5,1,4,2,0,3:T(2,128)S(1)}, f32[12,2,3,1,7,128]{5,1,4,2,0,3:T(2,128)}, u32[]{:S(2)}) copy-start(f32[12,2,3,1,7,128]{5,1,4,2,0,3:T(2,128)} %slice.327) | copy-start | bytes 774148
  480.2 12.7 %copy-start.60 = (f32[12,2,3,1,1,128]{5,1,4,2,0,3:T(2,128)S(1)}, f32[12,2,3,1,1,128]{5,1,4,2,0,3:T(2,128)}, u32[]{:S(2)}) copy-start(f32[12,2,3,1,1,128]{5,1,4,2,0,3:T(2,128)} %slice.326) | copy-start | bytes 110596
  480.2 12.7 %copy-start.95 = (f32[4,2,1,1,1]{0,1,4,3,2:T(2,128)S(1)}, f32[4,2,1,1,1]{0,1,4,3,2:T(2,128)}, u32[]{:S(2)}) copy-start(f32[4,2,1,1,1]{0,1,4,3,2:T(2,128)} %constant.108) | copy-start | bytes 100
  480.2 16.1 %copy-start.83 = (f32[4,2,1,1,1]{0,1,4,3,2:T(2,128)S(1)}, f32[4,2,1,1,1]{0,1,4,3,2:T(2,128)}, u32[]{:S(2)}) copy-start(f32[4,2,1,1,1]{0,1,4,3,2:T(2,128)} %constant.115) | copy-start | bytes 100
  526.2 15.0 %copy-start.88 = (f32[2,4,1,1,1]{1,0,4,3,2:T(2,128)S(1)}, f32[2,4,1,1,1]{1,0,4,3,2:T(2,128)}, u32[]{:S(2)}) copy-start(f32[2,4,1,1,1]{1,0,4,3,2:T(2,128)} %constant.97) | copy-start | bytes 100
  622.6 14.9 %copy-start.94 = (f32[4,2,1,1,1]{0,1,4,3,2:T(2,128)S(1)}, f32[4,2,1,1,1]{0,1,4,3,2:T(2,128)}, u32[]{:S(2)}) copy-start(f32[4,2,1,1,1]{0,1,4,3,2:T(2,128)} %constant.99) | copy-start | bytes 100
  (94 other events, 716.8 us)
Sparse Core Ops, SparseCore 0:
  680.1 88.6 all-reduce.2
where the time goes:
time: 785 us; the launch traced here: 777 us
  matrix products  411 us (52%)
  local copies, waits for them, and re-layouts  227 us (29%)
  waiting for transfers between devices  86.5 us (11%)
  other arithmetic  30.4 us (4%)
  between operations  16.8 us (2%)
    dot_general x92, matrix products, contract(): return jnp.einsum(form, left, right, precision=lax.Precision.HIGHEST)  399 us
    another operation x29, local copies, waits for them, and re-layouts  108 us
    unnamed x2, waiting for transfers between devices  86.5 us
    unnamed x242, local copies, waits for them, and re-layouts  21.3 us
    another operation x8, local copies, waits for them, and re-layouts, to_half(): stacked = jnp.stack([real_part, imag_part]).astype(jnp.bfloat16)  20.3 us
    concatenate x4, local copies, waits for them, and re-layouts, move(): rolled = jnp.roll(split, -step, axis=-1)  16.2 us
  transfers between devices with their start and end apart: 4, of which 1 were waited for; matrix products, arithmetic and copies ran while one was open for 72% of the time, Pallas kernels for 0%

commit v1 on v0

v1 whole, which is shorter than its diff:
```python
import functools
import jax
import jax.numpy as jnp
from jax import lax
from jax.experimental import pallas as pl
from jax.experimental.pallas import tpu as pltpu
from jax.sharding import PartitionSpec as P

VECTORS = 12
CT = 16
AGG_DEV = 4
BLOCK_SITES = 8
CHUNK = 3
CHUNKS = VECTORS // CHUNK
LANES = 256
MESH = pl.DeviceIdType.MESH
F32 = jnp.float32
BF16 = jnp.bfloat16

BACK = (
    ((1, (0, 1)), (0, (0, 1))),
    ((1, (1, 0)), (0, (-1, 0))),
    ((0, (0, 1)), (1, (0, -1))),
    ((0, (1, 0)), (1, (1, 0))),
)


def plus(base, factor, value):
    real, imag = factor
    if real:
        if real > 0:
            return (base[0] + value[0], base[1] + value[1])
        return (base[0] - value[0], base[1] - value[1])
    if imag > 0:
        return (base[0] - value[1], base[1] + value[0])
    return (base[0] + value[1], base[1] - value[0])


def flip(factor):
    return (-factor[0], -factor[1])


def project(mu, sign, field):
    out = []
    for row in range(2):
        column, factor = BACK[mu][row]
        if (sign > 0) != (mu == 3):
            factor = flip(factor)
        out.append([plus(field[row][a], factor, field[2 + column][a]) for a in range(3)])
    return out


def rebuild(mu, sign, total, half):
    for row in range(2):
        for a in range(3):
            total[row][a] = plus(total[row][a], (1, 0), half[row][a])
        column, factor = BACK[mu][row]
        if sign < 0:
            factor = flip(factor)
        for a in range(3):
            total[2 + row][a] = plus(total[2 + row][a], factor, half[column][a])
    return total


def color(link, dagger, half):
    out = []
    for row in half:
        line = []
        for a in range(3):
            real = imag = None
            for b in range(3):
                fr, fi = row[b]
                if dagger:
                    ur, ui = link(b, a)
                    r, i = ur * fr + ui * fi, ur * fi - ui * fr
                else:
                    ur, ui = link(a, b)
                    r, i = ur * fr - ui * fi, ur * fi + ui * fr
                real = r if real is None else real + r
                imag = i if imag is None else imag + i
            line.append((real, imag))
        out.append(line)
    return out


def rounded(half):
    flat = [part for row in half for pair in row for part in pair]
    flat = [part.astype(BF16).astype(F32) for part in flat]
    return unflatten(flat)


def unflatten(flat):
    return [[(flat[(s * 3 + a) * 2], flat[(s * 3 + a) * 2 + 1]) for a in range(3)] for s in range(len(flat) // 6)]


def mapped(half, function):
    return [[(function(p[0]), function(p[1])) for p in row] for row in half]


def rows_of(block, count):
    return [block[8 * i : 8 * i + 8] for i in range(count)]


def gathered(values, level=4):
    if len(values) == 1:
        return values[0]
    low = (lax.broadcasted_iota(jnp.int32, values[0].shape, 0) & level) == 0
    half = len(values) // 2
    out = []
    for i in range(half):
        a, b = values[i], values[i + half]
        kept = jnp.where(low, a, b)
        other = jnp.where(low, b, a)
        if level == 4:
            moved = pltpu.roll(other, 4, axis=0)
        else:
            moved = jnp.where(low, pltpu.roll(other, 8 - level, axis=0), pltpu.roll(other, level, axis=0))
        out.append(kept + moved)
    return gathered(out, level // 2)


def kernel(
    n_space, v_ref, u_ref, c_ref, owner_ref, agg_ref, applied_ref, coarse_ref,
    vf, uf, cf, acc, low_out, high_out, low_in, high_in, pairs, terms_out, terms_in,
    low_send, low_recv, high_send, high_recv, term_send, term_recv,
):
    part = lax.axis_index("parts")
    me = lax.axis_index("space")
    above = lax.rem(me + 1, n_space)
    below = lax.rem(me + n_space - 1, n_space)
    barrier = pltpu.get_barrier_semaphore()

    @pl.loop(1, n_space)
    def _(step):
        peer = lax.rem(me + step, n_space)
        pl.semaphore_signal(barrier, inc=1, device_id=(part, peer), device_id_type=MESH)

    lanes = lax.broadcasted_iota(jnp.int32, (8, 128), 1)
    last_time = (lanes & (CT - 1)) == CT - 1
    first_time = (lanes & (CT - 1)) == 0

    for c in range(2):
        for i in range(18):
            for j, block in enumerate(rows_of(u_ref[c, 16 * i : 16 * i + 16, :].astype(F32), 2)):
                at = 2 * i + j
                if at >= 27:
                    block = jnp.where(last_time, -block, block)
                uf[c, at] = block

    def link(mu):
        return lambda a, b: (uf[0, mu * 9 + a * 3 + b], uf[1, mu * 9 + a * 3 + b])

    def field_of(k):
        return [[(vf[0, k, s * 3 + a], vf[1, k, s * 3 + a]) for a in range(3)] for s in range(4)]

    def put_half(ref, k, half):
        flat = [half[s][a][c] for c in range(2) for s in range(2) for a in range(3)]
        for i in range(6):
            both = jnp.concatenate([flat[2 * i], flat[2 * i + 1]], axis=0)
            ref[k, 16 * i : 16 * i + 16, :] = both.astype(BF16)

    def get_half(ref, k):
        flat = []
        for i in range(6):
            flat += rows_of(ref[k, 16 * i : 16 * i + 16, :].astype(F32), 2)
        return [[(flat[s * 3 + a], flat[6 + s * 3 + a]) for a in range(3)] for s in range(2)]

    def halo(chunk):
        at = pl.ds(chunk * CHUNK, CHUNK)
        down = pltpu.make_async_remote_copy(
            src_ref=low_out.at[at], dst_ref=low_in.at[at],
            send_sem=low_send.at[chunk], recv_sem=low_recv.at[chunk],
            device_id=(part, below), device_id_type=MESH)
        up = pltpu.make_async_remote_copy(
            src_ref=high_out.at[at], dst_ref=high_in.at[at],
            send_sem=high_send.at[chunk], recv_sem=high_recv.at[chunk],
            device_id=(part, above), device_id_type=MESH)
        return down, up

    def first(k):
        for c in range(2):
            for i in range(6):
                for j, block in enumerate(rows_of(v_ref[c, k, 16 * i : 16 * i + 16, :].astype(F32), 2)):
                    vf[c, k, 2 * i + j] = block
        field = field_of(k)
        put_half(low_out, k, project(0, -1, field))
        put_half(high_out, k, color(link(0), True, project(0, 1, field)))

    def first_chunk(chunk):
        @pl.loop(0, CHUNK)
        def _(i):
            first(chunk * CHUNK + i)

    for chunk in range(CHUNKS):
        first_chunk(chunk)
        if chunk == 0:
            pl.semaphore_wait(barrier, n_space - 1)
        for copy in halo(chunk):
            copy.start()

    for c in range(2):
        for i in range(36):
            for j, block in enumerate(rows_of(c_ref[c, 16 * i : 16 * i + 16, :].astype(F32), 2)):
                cf[c, 2 * i + j] = block

    def ahead(mu, x):
        if mu == 1:
            return pltpu.roll(x, 7, axis=0)
        if mu == 2:
            return pltpu.roll(x, 128 - CT, axis=1)
        return jnp.where(last_time, pltpu.roll(x, CT - 1, axis=1), pltpu.roll(x, 127, axis=1))

    def behind(mu, x):
        if mu == 1:
            return pltpu.roll(x, 1, axis=0)
        if mu == 2:
            return pltpu.roll(x, CT, axis=1)
        return jnp.where(first_time, pltpu.roll(x, 128 - CT + 1, axis=1), pltpu.roll(x, 1, axis=1))

    @pl.loop(0, VECTORS)
    def _(k):
        total = None
        for mu in range(1, 4):
            field = field_of(k)
            lowered = mapped(rounded(project(mu, -1, field)), functools.partial(ahead, mu))
            forward = color(link(mu), False, lowered)
            raised = rounded(color(link(mu), True, project(mu, 1, field)))
            backward = mapped(raised, functools.partial(behind, mu))
            if total is None:
                zero = jnp.zeros((8, 128), F32)
                total = [[(zero, zero) for _ in range(3)] for _ in range(4)]
            total = rebuild(mu, -1, total, forward)
            total = rebuild(mu, 1, total, backward)
        field = field_of(k)
        for h in range(2):
            for row in range(6):
                real = imag = None
                for column in range(6):
                    at = h * 36 + row * 6 + column
                    cr, ci = cf[0, at], cf[1, at]
                    fr, fi = field[2 * h + column // 3][column % 3]
                    r, i = cr * fr - ci * fi, cr * fi + ci * fr
                    real = r if real is None else real + r
                    imag = i if imag is None else imag + i
                s, a = 2 * h + row // 3, row % 3
                fr, fi = field[s][a]
                tr, ti = total[s][a]
                acc[0, k, s * 3 + a] = 4.0 * fr + real - 0.5 * tr
                acc[1, k, s * 3 + a] = 4.0 * fi + imag - 0.5 * ti

    def finish(j):
        forward = color(link(0), False, get_half(low_in, j))
        backward = get_half(high_in, j)
        zero = jnp.zeros((8, 128), F32)
        total = [[(zero, zero) for _ in range(3)] for _ in range(4)]
        total = rebuild(0, -1, total, forward)
        total = rebuild(0, 1, total, backward)
        right = [[], []]
        for c in range(2):
            for i in range(6):
                both = []
                for at in (2 * i, 2 * i + 1):
                    both.append(acc[c, j, at] - 0.5 * total[at // 3][at % 3][c])
                both = jnp.concatenate(both, axis=0).astype(BF16)
                applied_ref[c, j, 16 * i : 16 * i + 16, :] = both
                right[c] += rows_of(both.astype(F32), 2)
        sums = [[], []]
        for k in range(VECTORS):
            real = imag = None
            for at in range(12):
                vr, vi = vf[0, k, at], vf[1, k, at]
                ar, ai = right[0][at], right[1][at]
                r, i = vr * ar + vi * ai, vr * ai - vi * ar
                real = r if real is None else real + r
                imag = i if imag is None else imag + i
            sums[0].append(real)
            sums[1].append(imag)
        flat = sums[0] + sums[1]
        for g in range(3):
            pairs[j, 8 * g : 8 * g + 8, :] = gathered(flat[8 * g : 8 * g + 8])

    for chunk in range(CHUNKS):
        for copy in halo(chunk):
            copy.wait_recv()

        @pl.loop(0, CHUNK)
        def _(i, chunk=chunk):
            finish(chunk * CHUNK + i)

    targets = owner_ref[...] * AGG_DEV + agg_ref[...]
    rows = lax.broadcasted_iota(jnp.int32, (8 * n_space, 128), 0)
    wanted = (rows >> 3) * AGG_DEV + (rows & (AGG_DEV - 1))
    named = targets == wanted
    width = VECTORS * VECTORS
    total = jnp.zeros((8 * n_space, width), F32)
    for half in range(2):
        select = jnp.where(named & (((rows >> 2) & 1) == half), 1.0, 0.0).astype(BF16)
        block = pairs[6 * half : 6 * half + 6].reshape(width, 128)
        large = block.astype(BF16)
        rest = block - large.astype(F32)
        middle = rest.astype(BF16)
        small = (rest - middle.astype(F32)).astype(BF16)
        for piece in (large, middle, small):
            total = total + lax.dot_general(
                select, piece, (((1,), (1,)), ((), ())), preferred_element_type=F32)
    terms_out[:, :, 0:width] = (total * (1.0 / (12.0 * BLOCK_SITES))).reshape(n_space, 8, width)
    terms_out[:, :, width:] = jnp.zeros((n_space, 8, LANES - width), F32)

    def term(peer, slot):
        return pltpu.make_async_remote_copy(
            src_ref=terms_out.at[peer], dst_ref=terms_in.at[slot],
            send_sem=term_send.at[peer], recv_sem=term_recv.at[slot],
            device_id=(part, peer), device_id_type=MESH)

    @pl.loop(1, n_space)
    def _(step):
        term(lax.rem(me + step, n_space), me).start()

    coarse_ref[...] = terms_out[me]

    @pl.loop(1, n_space)
    def _(step):
        peer = lax.rem(me + step, n_space)
        term(peer, peer).wait_recv()
        coarse_ref[...] += terms_in[peer]

    @pl.loop(1, n_space)
    def _(step):
        term(lax.rem(me + step, n_space), me).wait_send()

    for chunk in range(CHUNKS):
        for copy in halo(chunk):
            copy.wait_send()


def body(n_space, vectors, links, clover, block_owner, block_aggregate):
    v = vectors.reshape(2, VECTORS, 96, 128)
    u = links.reshape(2, 288, 128)
    c = clover.reshape(2, 576, 128)
    owner = block_owner.reshape(1, 128)
    aggregate = block_aggregate.reshape(1, 128)
    half = (VECTORS, 96, 128)
    applied, coarse = pl.pallas_call(
        functools.partial(kernel, n_space),
        out_shape=(
            jax.ShapeDtypeStruct(v.shape, BF16),
            jax.ShapeDtypeStruct((8, LANES), F32),
        ),
        in_specs=[pl.BlockSpec(memory_space=pltpu.VMEM)] * 5,
        out_specs=(pl.BlockSpec(memory_space=pltpu.VMEM),) * 2,
        scratch_shapes=[
            pltpu.VMEM((2, VECTORS, 12, 8, 128), F32),
            pltpu.VMEM((2, 36, 8, 128), F32),
            pltpu.VMEM((2, 72, 8, 128), F32),
            pltpu.VMEM((2, VECTORS, 12, 8, 128), F32),
            pltpu.VMEM(half, BF16),
            pltpu.VMEM(half, BF16),
            pltpu.VMEM(half, BF16),
            pltpu.VMEM(half, BF16),
            pltpu.VMEM((VECTORS, 24, 128), F32),
            pltpu.VMEM((n_space, 8, LANES), F32),
            pltpu.VMEM((n_space, 8, LANES), F32),
            pltpu.SemaphoreType.DMA((CHUNKS,)),
            pltpu.SemaphoreType.DMA((CHUNKS,)),
            pltpu.SemaphoreType.DMA((CHUNKS,)),
            pltpu.SemaphoreType.DMA((CHUNKS,)),
            pltpu.SemaphoreType.DMA((n_space,)),
            pltpu.SemaphoreType.DMA((n_space,)),
        ],
        compiler_params=pltpu.CompilerParams(
            collective_id=0, has_side_effects=True, vmem_limit_bytes=32 * 1024 * 1024
        ),
    )(v, u, c, owner, aggregate)
    coarse = coarse[:, : VECTORS * VECTORS].reshape(2, AGG_DEV, 6, 2, VECTORS)
    coarse = jnp.transpose(coarse, (1, 3, 4, 0, 2)).reshape(AGG_DEV, 2, VECTORS, VECTORS)
    return (applied.reshape(vectors.shape), coarse)


def solution(mesh):
    return jax.shard_map(
        functools.partial(body, mesh.shape["space"]),
        mesh=mesh,
        in_specs=(
            P(None, None, None, None, ("parts", "space"), None, None),
            P(None, None, None, None, ("parts", "space"), None, None),
            P(None, None, None, None, ("parts", "space"), None, None),
            P(("parts", "space"), None),
            P(("parts", "space")),
        ),
        out_specs=(
            P(None, None, None, None, ("parts", "space"), None, None),
            P(("parts", "space"), None, None, None),
        ),
        check_vma=False,
    )
```

time: 785 us -> 25.1 us (0.03)
  matrix products: 411 us -> 0 us
  local copies, waits for them, and re-layouts: 227 us -> 5.26 us
  waiting for transfers between devices: 86.5 us -> 0 us
  other arithmetic: 30.4 us -> 0 us
  Pallas kernels: 0 us -> 19 us
  between operations: 16.8 us -> 0.67 us
    dot_general x97 -> x0, matrix products: 411 us -> none  [the longest x92 399 us: contract(): return jnp.einsum(form, left, right, precision=lax.Precision.HIGHEST)]
    another operation x47 -> x0, local copies, waits for them, and re-layouts: 144 us -> none
    unnamed x2 -> x0, waiting for transfers between devices: 86.5 us -> none
    concatenate x6 -> x0, local copies, waits for them, and re-layouts: 27.4 us -> none  [the longest x4 16.2 us: move(): rolled = jnp.roll(split, -step, axis=-1)]
    pallas_call x0 -> x1, Pallas kernels: none -> 19 us  [body(): pl.pallas_call(functools.partial(kernel, n_space), out_shape=(jax.ShapeDt...]
    concatenate x8 -> x0, other arithmetic: 18.3 us -> none  [the longest x4 9.65 us: move(): rolled = jnp.roll(split, -step, axis=-2)]
    slice x30 -> x0, local copies, waits for them, and re-layouts: 17.4 us -> none  [the longest x8 5.99 us: move(): rolled = jnp.roll(split, -step, axis=-2)]
    unnamed x242 -> x12, local copies, waits for them, and re-layouts: 21.3 us -> 5.15 us
  transfers between devices with their start and end apart: 4 -> 0, of which waited for: 1 -> 0; matrix products, arithmetic and copies ran while one was open for 72% -> 0% of each run, Pallas kernels for 0% -> 0%
where the time goes in v1:
time: 25.1 us; the launch traced here: 24.9 us
  Pallas kernels  19 us (76%)
  local copies, waits for them, and re-layouts  5.26 us (21%)
  between operations  0.67 us (3%)
    pallas_call x1, Pallas kernels, body(): pl.pallas_call(functools.partial(kernel, n_space), out_shape=(jax.ShapeDt...  19 us
    unnamed x12, local copies, waits for them, and re-layouts  5.15 us

profile of v1, /device:TPU:0, one launch (start us, length us, event | category | flops | bytes accessed | tf_op | source)
XLA Modules:
  0.0 24.9 jit_solution(4108085003550863320)
XLA Ops:
  0.6 0.0 copy-start.3
  0.6 0.0 copy-start.4
  0.7 0.6 %copy-done.3 = s32[128,1]{0,1:T(1,128)S(1)} copy-done((s32[128,1]{0,1:T(1,128)S(1)}, s32[128,1]{0,1:T(1,128)}, u32[]{:S(2)}) %copy-start.3) | copy-done | bytes 536
  1.3 0.0 copy-done.4
  1.3 0.0 copy-start
  1.3 1.1 %copy-done = bf16[2,12,4,3,1,8,128]{6,5,4,3,2,1,0:T(8,128)(2,1)S(1)} copy-done((bf16[2,12,4,3,1,8,128]{6,5,4,3,2,1,0:T(8,128)(2,1)S(1)}, bf16[2,12,4,3,1,8,128]{6,5,4,3,2,1,0:T(8,128)(2,1)}, u32[]{:S(2)}) %copy-start) | copy-done | bytes 589848
  2.4 0.0 copy-start.1
  2.4 1.0 %copy-done.1 = bf16[2,2,6,6,1,8,128]{6,5,4,3,2,1,0:T(8,128)(2,1)S(1)} copy-done((bf16[2,2,6,6,1,8,128]{6,5,4,3,2,1,0:T(8,128)(2,1)S(1)}, bf16[2,2,6,6,1,8,128]{6,5,4,3,2,1,0:T(8,128)(2,1)}, u32[]{:S(2)}) %copy-start.1) | copy-done | bytes 294936
  3.3 0.0 copy-start.2
  3.3 0.9 %copy-done.2 = bf16[2,4,3,3,1,8,128]{6,5,4,3,2,1,0:T(8,128)(2,1)S(1)} copy-done((bf16[2,4,3,3,1,8,128]{6,5,4,3,2,1,0:T(8,128)(2,1)S(1)}, bf16[2,4,3,3,1,8,128]{6,5,4,3,2,1,0:T(8,128)(2,1)}, u32[]{:S(2)}) %copy-start.2) | copy-done | bytes 147480
  4.2 19.0 %shard_map.68 = (bf16[2,12,96,128]{3,2,1,0:T(8,128)(2,1)S(1)}, f32[8,256]{1,0:T(8,128)S(1)}) custom-call(bf16[2,12,96,128]{3,2,1,0:T(8,128)(2,1)S(1)} %bitcast.12, bf16[2,288,128]{2,1,0:T(8,128)(2,1)S(1)} %bitcast.15, bf16[2,576,128]{2,1,0:T(8,128)(2,1)S(1)} %bitcast.14, s32[1,128]{1,0:T(1,128)S(1)} %bitcast.17, s32[1,128]{1,0:T(1,128)S(1)} %bitcast.18), custom_call_target="tpu_custom_call" | custom-call | tf_op jit(solution)/shard_map/pallas_call | solution.py:343
  23.2 0.1 reshape.34
  23.3 0.7 %copy.11 = f32[4,2,12,12]{3,1,2,0:T(2,128)} copy(f32[4,2,12,12]{2,1,3,0:T(2,128)S(1)} %bitcast.19) | data formatting | bytes 9216
  24.1 0.8 %copy.13 = bf16[2,12,4,3,1,8,128]{6,5,4,3,2,1,0:T(8,128)(2,1)} copy(bf16[2,12,4,3,1,8,128]{6,5,4,3,2,1,0:T(8,128)(2,1)S(1)} %bitcast.13) | data formatting | bytes 1179648
  (1 shorter events, 0.0 us)
Async XLA Ops:
  0.6 0.7 %copy-start.3 = (s32[128,1]{0,1:T(1,128)S(1)}, s32[128,1]{0,1:T(1,128)}, u32[]{:S(2)}) copy-start(s32[128,1]{0,1:T(1,128)} %param.8) | copy-start | bytes 1540
  0.6 0.7 %copy-start.4 = (s32[128]{0:T(128)S(1)}, s32[128]{0:T(128)}, u32[]{:S(2)}) copy-start(s32[128]{0:T(128)} %param.9) | copy-start | bytes 1540
  1.3 1.1 %copy-start = (bf16[2,12,4,3,1,8,128]{6,5,4,3,2,1,0:T(8,128)(2,1)S(1)}, bf16[2,12,4,3,1,8,128]{6,5,4,3,2,1,0:T(8,128)(2,1)}, u32[]{:S(2)}) copy-start(bf16[2,12,4,3,1,8,128]{6,5,4,3,2,1,0:T(8,128)(2,1)} %param.5) | copy-start | bytes 1769476
  2.4 1.0 %copy-start.1 = (bf16[2,2,6,6,1,8,128]{6,5,4,3,2,1,0:T(8,128)(2,1)S(1)}, bf16[2,2,6,6,1,8,128]{6,5,4,3,2,1,0:T(8,128)(2,1)}, u32[]{:S(2)}) copy-start(bf16[2,2,6,6,1,8,128]{6,5,4,3,2,1,0:T(8,128)(2,1)} %param.7) | copy-start | bytes 884740
  3.3 0.9 %copy-start.2 = (bf16[2,4,3,3,1,8,128]{6,5,4,3,2,1,0:T(8,128)(2,1)S(1)}, bf16[2,4,3,3,1,8,128]{6,5,4,3,2,1,0:T(8,128)(2,1)}, u32[]{:S(2)}) copy-start(bf16[2,4,3,3,1,8,128]{6,5,4,3,2,1,0:T(8,128)(2,1)} %param.6) | copy-start | bytes 442372

commit v2 on v1

--- a/solution.py
+++ b/solution.py
@@ -10,9 +10,9 @@
 CT = 16
 AGG_DEV = 4
 BLOCK_SITES = 8
-CHUNK = 3
+CHUNK = 2
 CHUNKS = VECTORS // CHUNK
-LANES = 256
+WIDTH = 96
 MESH = pl.DeviceIdType.MESH
 F32 = jnp.float32
 BF16 = jnp.bfloat16
@@ -120,8 +120,9 @@
 
 
 def kernel(
-    n_space, v_ref, u_ref, c_ref, owner_ref, agg_ref, applied_ref, coarse_ref,
-    vf, uf, cf, acc, low_out, high_out, low_in, high_in, pairs, terms_out, terms_in,
+    n_space, v_hbm, u_hbm, c_hbm, owner_hbm, agg_hbm, applied_ref, coarse_ref,
+    v_ref, u_ref, c_ref, owner_ref, agg_ref, vf, uf, cf, acc, low_out, high_out, low_in, high_in, pairs, terms, terms_out, terms_in,
+    v_sem, u_sem, c_sem, owner_sem, agg_sem,
     low_send, low_recv, high_send, high_recv, term_send, term_recv,
 ):
     part = lax.axis_index("parts")
@@ -130,6 +131,22 @@
     below = lax.rem(me + n_space - 1, n_space)
     barrier = pltpu.get_barrier_semaphore()
 
+    u_load = pltpu.make_async_copy(u_hbm, u_ref, u_sem)
+    c_load = pltpu.make_async_copy(c_hbm, c_ref, c_sem)
+    owner_load = pltpu.make_async_copy(owner_hbm, owner_ref, owner_sem)
+    agg_load = pltpu.make_async_copy(agg_hbm, agg_ref, agg_sem)
+    v_loads = [
+        pltpu.make_async_copy(
+            v_hbm.at[:, pl.ds(chunk * CHUNK, CHUNK)], v_ref.at[:, pl.ds(chunk * CHUNK, CHUNK)], v_sem.at[chunk])
+        for chunk in range(CHUNKS)
+    ]
+    u_load.start()
+    for load in v_loads:
+        load.start()
+    c_load.start()
+    owner_load.start()
+    agg_load.start()
+
     @pl.loop(1, n_space)
     def _(step):
         peer = lax.rem(me + step, n_space)
@@ -139,13 +156,16 @@
     last_time = (lanes & (CT - 1)) == CT - 1
     first_time = (lanes & (CT - 1)) == 0
 
-    for c in range(2):
-        for i in range(18):
+    def unpack_links(begin, end):
+        for c, i in [(c, i) for c in range(2) for i in range(begin, end)]:
             for j, block in enumerate(rows_of(u_ref[c, 16 * i : 16 * i + 16, :].astype(F32), 2)):
                 at = 2 * i + j
                 if at >= 27:
                     block = jnp.where(last_time, -block, block)
                 uf[c, at] = block
+
+    u_load.wait()
+    unpack_links(0, 5)
 
     def link(mu):
         return lambda a, b: (uf[0, mu * 9 + a * 3 + b], uf[1, mu * 9 + a * 3 + b])
@@ -192,12 +212,15 @@
             first(chunk * CHUNK + i)
 
     for chunk in range(CHUNKS):
+        v_loads[chunk].wait()
         first_chunk(chunk)
         if chunk == 0:
             pl.semaphore_wait(barrier, n_space - 1)
         for copy in halo(chunk):
             copy.start()
 
+    unpack_links(5, 18)
+    c_load.wait()
     for c in range(2):
         for i in range(36):
             for j, block in enumerate(rows_of(c_ref[c, 16 * i : 16 * i + 16, :].astype(F32), 2)):
@@ -279,32 +302,43 @@
         for g in range(3):
             pairs[j, 8 * g : 8 * g + 8, :] = gathered(flat[8 * g : 8 * g + 8])
 
-    for chunk in range(CHUNKS):
-        for copy in halo(chunk):
-            copy.wait_recv()
-
-        @pl.loop(0, CHUNK)
-        def _(i, chunk=chunk):
-            finish(chunk * CHUNK + i)
-
+    owner_load.wait()
+    agg_load.wait()
     targets = owner_ref[...] * AGG_DEV + agg_ref[...]
-    rows = lax.broadcasted_iota(jnp.int32, (8 * n_space, 128), 0)
-    wanted = (rows >> 3) * AGG_DEV + (rows & (AGG_DEV - 1))
-    named = targets == wanted
-    width = VECTORS * VECTORS
-    total = jnp.zeros((8 * n_space, width), F32)
-    for half in range(2):
-        select = jnp.where(named & (((rows >> 2) & 1) == half), 1.0, 0.0).astype(BF16)
-        block = pairs[6 * half : 6 * half + 6].reshape(width, 128)
+    rows = lax.broadcasted_iota(jnp.int32, (16 * n_space, 128), 0)
+    named = targets == (rows >> 4) * AGG_DEV + (rows & (AGG_DEV - 1))
+    group = (rows >> 2) & 3
+
+    def reduce(g):
+        select = jnp.where(named & (group == g), 1.0, 0.0).astype(BF16)
+        block = pairs[4 * g : 4 * g + 4].reshape(WIDTH, 128)
         large = block.astype(BF16)
         rest = block - large.astype(F32)
         middle = rest.astype(BF16)
         small = (rest - middle.astype(F32)).astype(BF16)
+        total = None
         for piece in (large, middle, small):
-            total = total + lax.dot_general(
+            product = lax.dot_general(
                 select, piece, (((1,), (1,)), ((), ())), preferred_element_type=F32)
-    terms_out[:, :, 0:width] = (total * (1.0 / (12.0 * BLOCK_SITES))).reshape(n_space, 8, width)
-    terms_out[:, :, width:] = jnp.zeros((n_space, 8, LANES - width), F32)
+            total = product if total is None else total + product
+        return total
+
+    terms[:, WIDTH:] = jnp.zeros((16 * n_space, 128 - WIDTH), F32)
+    for chunk in range(CHUNKS):
+        for copy in halo(chunk):
+            copy.wait_recv()
+
+        @pl.loop(0, CHUNK)
+        def _(i, chunk=chunk):
+            finish(chunk * CHUNK + i)
+
+        done = (chunk + 1) * CHUNK
+        if done % 4 == 0:
+            if done == 4:
+                terms[:, 0:WIDTH] = reduce(0)
+            else:
+                terms[:, 0:WIDTH] += reduce(done // 4 - 1)
+    terms_out[...] = terms[...].astype(BF16).reshape(n_space, 16, 128)
 
     def term(peer, slot):
         return pltpu.make_async_remote_copy(
@@ -316,17 +350,20 @@
     def _(step):
         term(lax.rem(me + step, n_space), me).start()
 
-    coarse_ref[...] = terms_out[me]
+    mine = terms[pl.ds(pl.multiple_of(me * 16, 16), 16), :]
+    coarse_ref[...] = mine
 
     @pl.loop(1, n_space)
     def _(step):
         peer = lax.rem(me + step, n_space)
         term(peer, peer).wait_recv()
-        coarse_ref[...] += terms_in[peer]
+        coarse_ref[...] += terms_in[peer].astype(F32)
 
     @pl.loop(1, n_space)
     def _(step):
         term(lax.rem(me + step, n_space), me).wait_send()
+
+    coarse_ref[...] *= 1.0 / (12.0 * BLOCK_SITES)
 
     for chunk in range(CHUNKS):
         for copy in halo(chunk):
@@ -339,16 +376,23 @@
     c = clover.reshape(2, 576, 128)
     owner = block_owner.reshape(1, 128)
     aggregate = block_aggregate.reshape(1, 128)
+    v, u, c, owner, aggregate = [
+        pltpu.with_memory_space_constraint(x, pltpu.HBM) for x in (v, u, c, owner, aggregate)]
     half = (VECTORS, 96, 128)
     applied, coarse = pl.pallas_call(
         functools.partial(kernel, n_space),
         out_shape=(
             jax.ShapeDtypeStruct(v.shape, BF16),
-            jax.ShapeDtypeStruct((8, LANES), F32),
+            jax.ShapeDtypeStruct((16, 128), F32),
         ),
-        in_specs=[pl.BlockSpec(memory_space=pltpu.VMEM)] * 5,
+        in_specs=[pl.BlockSpec(memory_space=pltpu.HBM)] * 5,
         out_specs=(pl.BlockSpec(memory_space=pltpu.VMEM),) * 2,
         scratch_shapes=[
+            pltpu.VMEM(v.shape, BF16),
+            pltpu.VMEM(u.shape, BF16),
+            pltpu.VMEM(c.shape, BF16),
+            pltpu.VMEM((1, 128), jnp.int32),
+            pltpu.VMEM((1, 128), jnp.int32),
             pltpu.VMEM((2, VECTORS, 12, 8, 128), F32),
             pltpu.VMEM((2, 36, 8, 128), F32),
             pltpu.VMEM((2, 72, 8, 128), F32),
@@ -358,8 +402,14 @@
             pltpu.VMEM(half, BF16),
             pltpu.VMEM(half, BF16),
             pltpu.VMEM((VECTORS, 24, 128), F32),
-            pltpu.VMEM((n_space, 8, LANES), F32),
-            pltpu.VMEM((n_space, 8, LANES), F32),
+            pltpu.VMEM((16 * n_space, 128), F32),
+            pltpu.VMEM((n_space, 16, 128), BF16),
+            pltpu.VMEM((n_space, 16, 128), BF16),
+            pltpu.SemaphoreType.DMA((CHUNKS,)),
+            pltpu.SemaphoreType.DMA,
+            pltpu.SemaphoreType.DMA,
+            pltpu.SemaphoreType.DMA,
+            pltpu.SemaphoreType.DMA,
             pltpu.SemaphoreType.DMA((CHUNKS,)),
             pltpu.SemaphoreType.DMA((CHUNKS,)),
             pltpu.SemaphoreType.DMA((CHUNKS,)),
@@ -371,7 +421,7 @@
             collective_id=0, has_side_effects=True, vmem_limit_bytes=32 * 1024 * 1024
         ),
     )(v, u, c, owner, aggregate)
-    coarse = coarse[:, : VECTORS * VECTORS].reshape(2, AGG_DEV, 6, 2, VECTORS)
+    coarse = coarse[:12, :WIDTH].reshape(3, AGG_DEV, 4, 2, VECTORS)
     coarse = jnp.transpose(coarse, (1, 3, 4, 0, 2)).reshape(AGG_DEV, 2, VECTORS, VECTORS)
     return (applied.reshape(vectors.shape), coarse)
 

time: 25.1 us -> 21.5 us (0.86)
  local copies, waits for them, and re-layouts: 5.26 us -> 1.68 us
    unnamed x12 -> x2, local copies, waits for them, and re-layouts: 5.15 us -> 1.56 us
where the time goes in v2:
time: 21.5 us; the launch traced here: 21.3 us
  Pallas kernels  19 us (88%)
  local copies, waits for them, and re-layouts  1.68 us (8%)
  between operations  0.66 us (3%)
    pallas_call x1, Pallas kernels, body(): pl.pallas_call(functools.partial(kernel, n_space), out_shape=(jax.ShapeDt...  19 us
    unnamed x2, local copies, waits for them, and re-layouts  1.56 us

profile of v2, /device:TPU:0, one launch (start us, length us, event | category | flops | bytes accessed | tf_op | source)
XLA Modules:
  0.0 21.3 jit_solution(10036179575383030291)
XLA Ops:
  0.6 19.0 %shard_map.68 = (bf16[2,12,96,128]{3,2,1,0:T(8,128)(2,1)S(1)}, f32[16,128]{1,0:T(8,128)S(1)}) custom-call(bf16[2,12,96,128]{3,2,1,0:T(8,128)(2,1)} %bitcast.14, bf16[2,288,128]{2,1,0:T(8,128)(2,1)} %bitcast.17, bf16[2,576,128]{2,1,0:T(8,128)(2,1)} %bitcast.15, s32[1,128]{1,0:T(1,128)} %bitcast.18, s32[1,128]{1,0:T(1,128)} %bitcast.19), custom_call_target="tpu_custom_call" | custom-call | tf_op jit(solution)/shard_map/pallas_call | solution.py:382
  19.6 0.1 reshape.34
  19.8 0.7 %copy.11 = f32[4,2,12,12]{3,1,2,0:T(2,128)} copy(f32[4,2,12,12]{2,1,3,0:T(2,128)S(1)} %bitcast.16) | data formatting | bytes 9216
  20.5 0.8 %copy.13 = bf16[2,12,4,3,1,8,128]{6,5,4,3,2,1,0:T(8,128)(2,1)} copy(bf16[2,12,4,3,1,8,128]{6,5,4,3,2,1,0:T(8,128)(2,1)S(1)} %bitcast.12) | data formatting | bytes 1179648
  (1 shorter events, 0.0 us)
